TPU v7x, 32 devices: a whole 2x2x4 slice. The times are simulated.
32 devices in a mesh: groups: 2 (over y), band: 16 (over z, x, core).
Axes of the slice: x: 2, y: 2, z: 4, core: 2. Of those that a mesh axis runs over, the one named last changes fastest.
Arguments:
- grid_feats: bfloat16 [8192, 227], P(('groups', 'band')), parts along dimension 0, may hold values from -6 to 6
- mesh_feat: bfloat16 [4096, 512], P('band'), may hold values from -6 to 6
- edge_latent: bfloat16 [32768, 512], P('band'), may hold values from -6 to 6
- g2m_owner: int32 [4096, 1], P('band'), may hold values from 0 to 15; in each aligned block of 256 rows (0 to 255, 256 to 511, ...) at most 32 rows name the same one
- g2m_node: int32 [4096], P('band'), may hold values from 0 to 255
- edge_sender: int32 [32768], P('band'), may hold values from 0 to 319
- edge_receiver: int32 [32768], P('band'), may hold values from 0 to 255
- border_low: int32 [16, 32], P('band'), may hold values from 0 to 255
- border_high: int32 [16, 32], P('band'), may hold values from 0 to 255
- w_embed: bfloat16 [227, 512], replicated, may hold values from -0.375 to 0.375
- w_g2m: bfloat16 [512, 512], replicated, may hold values from -0.25 to 0.25
- gain_enc: float32 [512], replicated, may hold values from 0.1 to 1.9
- w_edge_in: bfloat16 [2, 1536, 512], replicated, may hold values from -0.15625 to 0.15625
- w_edge_out: bfloat16 [2, 512, 512], replicated, may hold values from -0.25 to 0.25
- gain_edge: float32 [2, 512], replicated, may hold values from 0.1 to 1.9
- w_node_in: bfloat16 [2, 1024, 512], replicated, may hold values from -0.1875 to 0.1875
- w_node_out: bfloat16 [2, 512, 512], replicated, may hold values from -0.25 to 0.25
- gain_node: float32 [2, 512], replicated, may hold values from 0.1 to 1.9
- w_m2g_mesh: bfloat16 [512, 512], replicated, may hold values from -0.25 to 0.25
- w_m2g_grid: bfloat16 [512, 512], replicated, may hold values from -0.25 to 0.25
- w_out: bfloat16 [512, 227], replicated, may hold values from -0.25 to 0.25
Outputs:
- prediction: bfloat16 [8192, 227], P(('groups', 'band')), parts along dimension 0
There are 2 independent parts, one for each index of `groups`. A program takes and returns all parts, laid end to end along the dimension named above; an argument that names none is the same for every part. Nothing has to cross between parts.
Inputs may be any that keep to these rules, and one draw needn't show every extreme that they name: `g2m_owner`: among the grid points of one partition at most 32 name the same owner, and in some partition one owner is named by exactly 32 of them. `edge_sender`: values below 256 name the partition's own nodes, the next 32 values the previous partition's high border list, the last 32 the next partition's low border list.
All inputs are finite; a program needn't handle non-finite values.
Results may differ from a plain program's by a relative error of at most 0.013.
Values may be sent and summed in bfloat16 or wider, within the bound.
A program may use at most 128 MiB of HBM per device.

v0:
```python
import jax
import jax.numpy as jnp
from jax import lax
from jax.sharding import PartitionSpec as P


def with_halo(shard, sides, width):
    for axis, dim in sides:
        size, length = (lax.axis_size(axis), shard.shape[dim])
        up = [(i, (i + 1) % size) for i in range(size - 1)]
        down = [(j, i) for i, j in up]
        last = lax.slice_in_dim(shard, length - width, length, axis=dim)
        leading = lax.slice_in_dim(shard, 0, width, axis=dim)
        before = lax.ppermute(last, axis, up)
        after = lax.ppermute(leading, axis, down)
        shard = jnp.concatenate([before, shard, after], axis=dim)
    return shard


def rms_norm(values, gain):
    return values * lax.rsqrt(jnp.mean(values * values, -1, keepdims=True) + 1e-05) * gain


def shards(
    grid_feats,
    mesh_feat,
    edge_latent,
    g2m_owner,
    g2m_node,
    edge_sender,
    edge_receiver,
    border_low,
    border_high,
    w_embed,
    w_g2m,
    gain_enc,
    w_edge_in,
    w_edge_out,
    gain_edge,
    w_node_in,
    w_node_out,
    gain_node,
    w_m2g_mesh,
    w_m2g_grid,
    w_out,
):
    f32 = jnp.float32
    bf16 = jnp.bfloat16
    part_count = lax.axis_size("band")
    grid_rows = grid_feats.shape[0]
    mesh_rows = mesh_feat.shape[0]
    latent_width = mesh_feat.shape[1]
    capacity = 2 * grid_rows // part_count
    grid_latent = jax.nn.silu(jnp.dot(grid_feats, w_embed, preferred_element_type=f32)).astype(bf16)
    owners = g2m_owner[:, 0]
    owner_hot = (owners[:, None] == jnp.arange(part_count, dtype=jnp.int32)[None, :]).astype(
        jnp.int32
    )
    slot_pos = jnp.sum(jnp.cumsum(owner_hot, 0) * owner_hot, 1) - 1
    flat_slot = owners * capacity + slot_pos
    send_ids = jnp.full((part_count * capacity,), -1, jnp.int32).at[flat_slot].set(g2m_node)
    send_rows = (
        jnp.zeros((part_count * capacity, latent_width), bf16).at[flat_slot].set(grid_latent)
    )
    recv_rows, recv_ids = (
        lax.all_to_all(
            send_rows.reshape(part_count, capacity, latent_width),
            "band",
            split_axis=0,
            concat_axis=0,
            tiled=True,
        ),
        lax.all_to_all(
            send_ids.reshape(part_count, capacity), "band", split_axis=0, concat_axis=0, tiled=True
        ),
    )
    slot_rows = recv_rows.reshape(-1, latent_width)
    slot_ids = recv_ids.reshape(-1)
    picker = (jnp.arange(mesh_rows, dtype=jnp.int32)[:, None] == slot_ids[None, :]).astype(bf16)
    encoded = jnp.dot(picker, slot_rows, preferred_element_type=f32).astype(bf16)
    mesh_state = (
        mesh_feat.astype(f32)
        + rms_norm(jnp.dot(encoded, w_g2m, preferred_element_type=f32), gain_enc)
    ).astype(bf16)
    border_rows = border_low.shape[1]
    low_nodes = border_low[0]
    high_nodes = border_high[0]
    edge_hot = (jnp.arange(mesh_rows, dtype=jnp.int32)[:, None] == edge_receiver[None, :]).astype(
        bf16
    )
    edges_now = edge_latent
    for depth in range(w_edge_in.shape[0]):
        rim_rows = jnp.concatenate([mesh_state[low_nodes], mesh_state[high_nodes]], 0)
        padded = with_halo(rim_rows, (("band", 0),), border_rows)
        sender_table = jnp.concatenate(
            [mesh_state, padded[:border_rows], padded[3 * border_rows :]], 0
        )
        edge_weight = w_edge_in[depth]
        from_sender = jnp.dot(
            sender_table, edge_weight[latent_width : 2 * latent_width], preferred_element_type=f32
        )
        from_receiver = jnp.dot(
            mesh_state, edge_weight[2 * latent_width :], preferred_element_type=f32
        )
        pre_act = (
            jnp.dot(edges_now, edge_weight[:latent_width], preferred_element_type=f32)
            + from_sender[edge_sender]
            + from_receiver[edge_receiver]
        )
        edge_hidden = jax.nn.silu(pre_act).astype(bf16)
        edges_now = (
            edges_now.astype(f32)
            + rms_norm(
                jnp.dot(edge_hidden, w_edge_out[depth], preferred_element_type=f32),
                gain_edge[depth],
            )
        ).astype(bf16)
        edge_sum = jnp.dot(edge_hot, edges_now, preferred_element_type=f32).astype(bf16)
        node_weight = w_node_in[depth]
        node_pre = jnp.dot(
            mesh_state, node_weight[:latent_width], preferred_element_type=f32
        ) + jnp.dot(edge_sum, node_weight[latent_width:], preferred_element_type=f32)
        node_hidden = jax.nn.silu(node_pre).astype(bf16)
        mesh_state = (
            mesh_state.astype(f32)
            + rms_norm(
                jnp.dot(node_hidden, w_node_out[depth], preferred_element_type=f32),
                gain_node[depth],
            )
        ).astype(bf16)
    safe_ids = jnp.maximum(slot_ids, 0)
    mesh_term = jnp.dot(mesh_state, w_m2g_mesh, preferred_element_type=f32).astype(bf16)
    reply_rows = mesh_term[safe_ids].reshape(part_count, capacity, latent_width)
    returned = lax.all_to_all(reply_rows, "band", split_axis=0, concat_axis=0, tiled=True)
    fetched = returned.reshape(-1, latent_width)[flat_slot]
    decoded = jax.nn.silu(
        fetched.astype(f32) + jnp.dot(grid_latent, w_m2g_grid, preferred_element_type=f32)
    ).astype(bf16)
    return (grid_feats.astype(f32) + jnp.dot(decoded, w_out, preferred_element_type=f32)).astype(
        bf16
    )


def solution(mesh):
    return jax.shard_map(
        shards,
        mesh=mesh,
        in_specs=(
            P(("groups", "band"), None),
            P("band", None),
            P("band", None),
            P("band", None),
            P("band"),
            P("band"),
            P("band"),
            P("band", None),
            P("band", None),
            P(),
            P(),
            P(),
            P(),
            P(),
            P(),
            P(),
            P(),
            P(),
            P(),
            P(),
            P(),
        ),
        out_specs=P(("groups", "band"), None),
        check_vma=False,
    )
```

profile of v0, /device:TPU:0, one launch (start us, length us, event | category | flops | bytes accessed | tf_op | source)
XLA Modules:
  0.0 164.6 jit_solution(2124773703145082546)
XLA Ops:
  0.0 0.7 fusion.86
  1.6 0.8 fusion.85
  2.3 0.7 compare_select_fusion.2
  3.0 1.6 scatter_custom_fusion
  4.6 0.7 all_to_all.12
  5.3 7.4 %all-to-all-start = ((s32[16,1,32]{2,1,0:T(1,128)}), s32[16,1,32]{2,1,0:T(1,128)S(1)}, u32[]{:S(2)}, u32[]{:S(2)}) async-start(s32[16,1,32]{2,1,0:T(1,128)} %all_to_all.12), calls=%async_computation | async-start | bytes 16384 | tf_op jit(solution)/shard_map/all_to_all | solution.py:73
  12.6 0.7 fusion.91
  13.3 0.7 fusion.92
  14.0 1.4 fusion.99
  15.3 1.2 fusion.104
  16.6 3.2 %copy.24 = bf16[2048,512]{0,1:T(8,128)(2,1)S(1)} copy(bf16[2048,512]{1,0:T(8,128)(2,1)} %param.23) | data formatting | bytes 4194304 | tf_op args[2]
  19.8 2.4 %scatter_custom_fusion.1 = bf16[512,512]{1,0:T(8,128)(2,1)} fusion(s32[256]{0:T(256)S(1)} %bitcast.125, bf16[]{:T(256)} %constant.21.clone.1, f32[256,512]{1,0:T(8,128)S(1)} %fusion.104), kind=kCustom, calls=%fused_computation.100 | custom fusion | flops 655360 | bytes 1048578 | tf_op jit(solution)/shard_map/scatter | solution.py:63
  22.2 6.1 %all-to-all-start.1 = ((bf16[16,32,512]{2,1,0:T(8,128)(2,1)}), bf16[16,32,512]{2,1,0:T(8,128)(2,1)}, u32[]{:S(2)}, u32[]{:S(2)}) async-start(bf16[16,32,512]{2,1,0:T(8,128)(2,1)} %bitcast.118), calls=%async_computation.1 | async-start | bytes 1048576 | tf_op jit(solution)/shard_map/all_to_all | solution.py:66
  29.4 0.7 maximum_reduce_fusion
  30.9 11.9 %all-to-all-done.1 = bf16[16,32,512]{2,1,0:T(8,128)(2,1)} async-done(((bf16[16,32,512]{2,1,0:T(8,128)(2,1)}), bf16[16,32,512]{2,1,0:T(8,128)(2,1)}, u32[]{:S(2)}, u32[]{:S(2)}) %all-to-all-start.1) | async-done | bytes 524320 | tf_op jit(solution)/shard_map/all_to_all | solution.py:66
  42.8 2.4 %multiply_reduce_fusion.4 = (f32[256]{0:T(256)S(1)}, f32[256,512]{1,0:T(8,128)}) fusion(bf16[512,512]{1,0:T(8,128)(2,1)S(1)} %copy-done, bf16[512,512]{1,0:T(8,128)(2,1)} %bitcast.6, s32[512]{0:T(512)S(1)} %eq.62), kind=kOutput, calls=%fused_computation.84 | convolution fusion | flops 268959488 | bytes 1575936 | tf_op jit(solution)/shard_map/dot_general | solution.py:83
  45.2 1.2 add_convert_fusion.11
  46.4 0.6 gather_fusion
  47.1 1.9 %collective-permute-start = (bf16[32,512]{1,0:T(8,128)(2,1)S(1)}, bf16[32,512]{1,0:T(8,128)(2,1)S(1)}, u32[]{:S(2)}, u32[]{:S(2)}) collective-permute-start(bf16[32,512]{1,0:T(8,128)(2,1)S(1)} %gather_fusion), channel_id=1, source_target_pairs={{0,1},{1,2},{2,3},{3,4},{4,5},{5,6},{6,7},{7,8},{8,9},{9,10},{10,1... | collective-permute-start | bytes 98312 | tf_op jit(solution)/shard_map/ppermute | solution.py:14
  49.0 0.6 gather_fusion.1
  49.6 1.3 collective-permute-start.1
  50.9 1.3 fusion.34
  52.3 2.1 %fusion.44 = f32[256,512]{1,0:T(8,128)} fusion(bf16[256,512]{1,0:T(8,128)(2,1)S(1)} %add_convert_fusion.11, bf16[2,1024,512]{2,1,0:T(8,128)(2,1)} %param.36), kind=kOutput, calls=%fused_computation.59 | convolution fusion | flops 134217728 | bytes 1310720 | tf_op jit(solution)/shard_map/dot_general | solution.py:120
  54.4 8.9 %gather_fusion.3 = f32[2048,512]{1,0:T(8,128)} fusion(f32[256,512]{1,0:T(8,128)S(1)} %fusion.34, s32[2048]{0:T(1024)S(1)} %fusion.88), kind=kCustom, calls=%fused_computation.3 | custom fusion | bytes 8396800 | tf_op jit(solution)/shard_map/gather | solution.py:108
  63.3 0.6 copy-done.26
  63.9 1.4 fusion.36
  65.4 8.9 %gather_fusion.2 = f32[2048,512]{1,0:T(8,128)} fusion(f32[320,512]{1,0:T(8,128)S(1)} %fusion.36, s32[2048]{0:T(1024)S(1)} %fusion.87), kind=kCustom, calls=%fused_computation.2 | custom fusion | bytes 8396800 | tf_op jit(solution)/shard_map/gather | solution.py:107
  74.3 9.1 %multiply_reduce_fusion.1 = (f32[2048]{0:T(1024)S(1)}, f32[2048,512]{0,1:T(8,128)}) fusion(bf16[2,512,512]{2,1,0:T(8,128)(2,1)} %param.34, f32[2048,512]{1,0:T(8,128)} %gather_fusion.3, f32[2048,512]{1,0:T(8,128)} %gather_fusion.2, bf16[2048,512]{1,0:T(8,128)(2,1)} %param.23, bf16[2,1536,512]{2,1,0:T(8,128)(2,1)} %param.33), kind=kOutput, calls=%fused_computation.16 | convolution fusion | flops 2156918784 | bytes 15736832 | tf_op jit(solution)/shard_map/dot_general | solution.py:114
  83.4 4.2 %add_convert_fusion.1 = bf16[2048,512]{0,1:T(8,128)(2,1)} fusion(f32[2048,512]{0,1:T(8,128)} %get-tuple-element.14, bf16[2048,512]{0,1:T(8,128)(2,1)S(1)} %copy.24, f32[512]{0:T(512)S(1)} %bitcast.123, f32[2048]{0:T(1024)S(1)} %add_rsqrt_fusion.1), kind=kLoop, calls=%fused_computation.15 | loop fusion | flops 5242880 | bytes 8398848 | tf_op jit(solution)/shard_map/convert_element_type | solution.py:117
  87.6 2.8 %multiply_convert_fusion.6 = bf16[256,512]{1,0:T(8,128)(2,1)S(1)} fusion(f32[256,512]{1,0:T(8,128)S(1)} %copy-done.5, bf16[2048,512]{0,1:T(8,128)(2,1)} %add_convert_fusion.1, s32[2048]{0:T(1024)S(1)} %copy-done.14, bf16[2,1024,512]{2,1,0:T(8,128)(2,1)} %param.36), kind=kOutput, calls=%fused_computation.76 | convolution fusion | flops 672530432 | bytes 3416064 | tf_op jit(solution)/shard_map/dot_general | solution.py:122
  91.0 0.7 gather_fusion.4
  91.8 0.7 gather_fusion.5
  92.5 1.3 fusion.18
  93.9 3.0 %collective-permute-start.2 = (bf16[32,512]{1,0:T(8,128)(2,1)S(1)}, bf16[32,512]{1,0:T(8,128)(2,1)S(1)}, u32[]{:S(2)}, u32[]{:S(2)}) collective-permute-start(bf16[32,512]{1,0:T(8,128)(2,1)S(1)} %gather_fusion.4), channel_id=1, source_target_pairs={{0,1},{1,2},{2,3},{3,4},{4,5},{5,6},{6,7},{7,8},{8,9},{9,10},{10,1... | collective-permute-start | bytes 98312 | tf_op jit(solution)/shard_map/ppermute | solution.py:14
  96.9 1.5 collective-permute-start.3
  98.4 2.1 %fusion.28 = f32[256,512]{1,0:T(8,128)} fusion(bf16[256,512]{1,0:T(8,128)(2,1)S(1)} %add_convert_fusion.10, bf16[2,1024,512]{2,1,0:T(8,128)(2,1)} %param.36), kind=kOutput, calls=%fused_computation.47 | convolution fusion | flops 134217728 | bytes 1310720 | tf_op jit(solution)/shard_map/dot_general | solution.py:120
  100.5 8.9 %gather_fusion.7 = f32[2048,512]{1,0:T(8,128)} fusion(f32[256,512]{1,0:T(8,128)S(1)} %fusion.18, s32[2048]{0:T(1024)S(1)} %fusion.88), kind=kCustom, calls=%fused_computation.7 | custom fusion | bytes 8396800 | tf_op jit(solution)/shard_map/gather | solution.py:108
  109.5 1.4 fusion.20
  110.9 8.9 %gather_fusion.6 = f32[2048,512]{1,0:T(8,128)} fusion(f32[320,512]{1,0:T(8,128)S(1)} %fusion.20, s32[2048]{0:T(1024)S(1)} %fusion.87), kind=kCustom, calls=%fused_computation.6 | custom fusion | bytes 8396800 | tf_op jit(solution)/shard_map/gather | solution.py:107
  119.8 8.7 %multiply_reduce_fusion = (f32[2048]{0:T(1024)S(1)}, f32[2048,512]{0,1:T(8,128)}) fusion(bf16[2,512,512]{2,1,0:T(8,128)(2,1)} %param.34, f32[2048,512]{1,0:T(8,128)} %gather_fusion.7, f32[2048,512]{1,0:T(8,128)} %gather_fusion.6, bf16[2048,512]{0,1:T(8,128)(2,1)S(1)} %copy-done.3, bf16[2,1536,512]{2,1,0:T(8,128)(2,1)} %param.33), kind=kOutput, calls=%fused_computation.13 | convolution fusion | flops 2156918784 | bytes 15736832 | tf_op jit(solution)/shard_map/dot_general | solution.py:114
  128.5 4.5 %multiply_convert_fusion.5 = bf16[256,512]{1,0:T(8,128)(2,1)} fusion(f32[256,512]{1,0:T(8,128)S(1)} %copy-done.6, f32[2048,512]{0,1:T(8,128)} %get-tuple-element.18, bf16[2048,512]{0,1:T(8,128)(2,1)S(1)} %copy-done.3, f32[512]{0:T(512)S(1)} %bitcast.128, f32[2048]{0:T(1024)S(1)} %add_rsqrt_fusion, s32[2048]{0:T(1024)S(1)} %copy-done.15, ...), kind=kOutput, calls=%fused_computation.66 | convolution fusion | flops 677773312 | bytes 7620608 | tf_op jit(solution)/shard_map/dot_general | solution.py:122
  133.0 1.5 multiply_reduce_fusion.2
  134.5 1.4 convolution_convert_fusion
  136.0 2.6 %gather_fusion.8 = bf16[512,512]{1,0:T(8,128)(2,1)} fusion(bf16[256,512]{1,0:T(8,128)(2,1)S(1)} %convolution_convert_fusion, s32[1024]{0:T(1024)S(1)} %copy-done.9), kind=kCustom, calls=%fused_computation.8 | custom fusion | bytes 1050624 | tf_op jit(solution)/shard_map/gather | solution.py:133
  138.6 9.0 %all-to-all-start.2 = ((bf16[16,32,512]{2,1,0:T(8,128)(2,1)}), bf16[16,32,512]{2,1,0:T(8,128)(2,1)S(1)}, u32[]{:S(2)}, u32[]{:S(2)}) async-start(bf16[16,32,512]{2,1,0:T(8,128)(2,1)} %bitcast.29), calls=%async_computation.2 | async-start | bytes 1048576 | tf_op jit(solution)/shard_map/all_to_all | solution.py:134
  147.7 14.4 %all-to-all-done.2 = bf16[16,32,512]{2,1,0:T(8,128)(2,1)S(1)} async-done(((bf16[16,32,512]{2,1,0:T(8,128)(2,1)}), bf16[16,32,512]{2,1,0:T(8,128)(2,1)S(1)}, u32[]{:S(2)}, u32[]{:S(2)}) %all-to-all-start.2) | async-done | bytes 524320 | tf_op jit(solution)/shard_map/all_to_all | solution.py:134
  162.1 1.2 gather_fusion.9
  163.3 1.3 fusion.9
  (80 shorter events, 3.3 us)
Async XLA Ops:
  0.0 42.8 %copy-start = (bf16[512,512]{1,0:T(8,128)(2,1)S(1)}, bf16[512,512]{1,0:T(8,128)(2,1)}, u32[]{:S(2)}) copy-start(bf16[512,512]{1,0:T(8,128)(2,1)} %param.31) | copy-start | bytes 1572868
  0.0 28.3 %copy-start.21 = (f32[2,512]{1,0:T(2,128)S(1)}, f32[2,512]{1,0:T(2,128)}, u32[]{:S(2)}) copy-start(f32[2,512]{1,0:T(2,128)} %param.38) | copy-start | bytes 12292
  0.0 28.9 %copy-start.12 = (s32[2048]{0:T(1024)S(1)}, s32[2048]{0:T(1024)}, u32[]{:S(2)}) copy-start(s32[2048]{0:T(1024)} %param.26) | copy-start | bytes 24580
  0.0 28.9 %copy-start.13 = (s32[2048]{0:T(1024)S(1)}, s32[2048]{0:T(1024)}, u32[]{:S(2)}) copy-start(s32[2048]{0:T(1024)} %param.27) | copy-start | bytes 24580
  3.0 42.2 %copy-start.19 = (s32[256,1]{0,1:T(1,128)}, s32[256,1]{0,1:T(1,128)S(1)}, u32[]{:S(2)}) copy-start(s32[256,1]{0,1:T(1,128)S(1)} %compare_select_fusion.2) | copy-start | bytes 3076
  5.3 17.0 %all-to-all-start = ((s32[16,1,32]{2,1,0:T(1,128)}), s32[16,1,32]{2,1,0:T(1,128)S(1)}, u32[]{:S(2)}, u32[]{:S(2)}) async-start(s32[16,1,32]{2,1,0:T(1,128)} %all_to_all.12), calls=%async_computation | async-start | bytes 16384 | tf_op jit(solution)/shard_map/all_to_all | solution.py:73
  16.6 28.6 %copy-start.1 = (f32[256,512]{1,0:T(8,128)}, f32[256,512]{1,0:T(8,128)S(1)}, u32[]{:S(2)}) copy-start(f32[256,512]{1,0:T(8,128)S(1)} %fusion.104) | copy-start | bytes 1572868
  16.6 28.6 %copy-start.7 = (bf16[256,512]{1,0:T(8,128)(2,1)S(1)}, bf16[256,512]{1,0:T(8,128)(2,1)}, u32[]{:S(2)}) copy-start(bf16[256,512]{1,0:T(8,128)(2,1)} %param.22) | copy-start | bytes 786436
  16.6 28.6 %copy-start.22 = (f32[512]{0:T(512)S(1)}, f32[512]{0:T(512)}, u32[]{:S(2)}) copy-start(f32[512]{0:T(512)} %param.32) | copy-start | bytes 6148
  16.6 29.8 %copy-start.17 = (s32[1024]{0:T(1024)}, s32[1024]{0:T(1024)S(1)}, u32[]{:S(2)}) copy-start(s32[1024]{0:T(1024)S(1)} %pad_clamp_fusion.3) | copy-start | bytes 12292
  22.2 20.6 %all-to-all-start.1 = ((bf16[16,32,512]{2,1,0:T(8,128)(2,1)}), bf16[16,32,512]{2,1,0:T(8,128)(2,1)}, u32[]{:S(2)}, u32[]{:S(2)}) async-start(bf16[16,32,512]{2,1,0:T(8,128)(2,1)} %bitcast.118), calls=%async_computation.1 | async-start | bytes 1048576 | tf_op jit(solution)/shard_map/all_to_all | solution.py:66
  28.3 35.0 %copy-start.18 = (s32[1024]{0:T(1024)}, s32[1024]{0:T(1024)S(1)}, u32[]{:S(2)}) copy-start(s32[1024]{0:T(1024)S(1)} %pad_clamp_fusion.2) | copy-start | bytes 12292
  47.1 16.3 %collective-permute-start = (bf16[32,512]{1,0:T(8,128)(2,1)S(1)}, bf16[32,512]{1,0:T(8,128)(2,1)S(1)}, u32[]{:S(2)}, u32[]{:S(2)}) collective-permute-start(bf16[32,512]{1,0:T(8,128)(2,1)S(1)} %gather_fusion), channel_id=1, source_target_pairs={{0,1},{1,2},{2,3},{3,4},{4,5},{5,6},{6,7},{7,8},{8,9},{9,10},{10,1... | collective-permute-start | bytes 98312 | tf_op jit(solution)/shard_map/ppermute | solution.py:14
  49.6 14.3 %collective-permute-start.1 = (bf16[32,512]{1,0:T(8,128)(2,1)S(1)}, bf16[32,512]{1,0:T(8,128)(2,1)}, u32[]{:S(2)}, u32[]{:S(2)}) collective-permute-start(bf16[32,512]{1,0:T(8,128)(2,1)S(1)} %gather_fusion.1), channel_id=1, source_target_pairs={{1,0},{2,1},{3,2},{4,3},{5,4},{6,5},{7,6},{8,7},{9,8},{10,9},{11,1... | collective-permute-start | bytes 98312 | tf_op jit(solution)/shard_map/ppermute | solution.py:15
  63.3 0.6 copy-start.26
  74.3 9.1 %copy-start.16 = (f32[1,512]{1,0:T(1,128)S(1)}, f32[1,512]{1,0:T(1,128)}, u32[]{:S(2)}) copy-start(f32[1,512]{1,0:T(1,128)} %get-tuple-element.10) | copy-start | bytes 6148
  83.4 4.3 %copy-start.5 = (f32[256,512]{1,0:T(8,128)S(1)}, f32[256,512]{1,0:T(8,128)}, u32[]{:S(2)}) copy-start(f32[256,512]{1,0:T(8,128)} %fusion.44) | copy-start | bytes 1572868
  83.4 4.2 %copy-start.14 = (s32[2048]{0:T(1024)S(1)}, s32[2048]{0:T(1024)}, u32[]{:S(2)}) copy-start(s32[2048]{0:T(1024)} %param.27) | copy-start | bytes 24580
  87.6 2.8 %copy-start.4 = (bf16[2,512,512]{2,1,0:T(8,128)(2,1)S(1)}, bf16[2,512,512]{2,1,0:T(8,128)(2,1)}, u32[]{:S(2)}) copy-start(bf16[2,512,512]{2,1,0:T(8,128)(2,1)} %param.37) | copy-start | bytes 3145732
  87.6 3.2 %copy-start.11 = (f32[1,512]{1,0:T(1,128)S(1)}, f32[1,512]{1,0:T(1,128)}, u32[]{:S(2)}) copy-start(f32[1,512]{1,0:T(1,128)} %get-tuple-element.8) | copy-start | bytes 6148
  93.9 15.6 %collective-permute-start.2 = (bf16[32,512]{1,0:T(8,128)(2,1)S(1)}, bf16[32,512]{1,0:T(8,128)(2,1)S(1)}, u32[]{:S(2)}, u32[]{:S(2)}) collective-permute-start(bf16[32,512]{1,0:T(8,128)(2,1)S(1)} %gather_fusion.4), channel_id=1, source_target_pairs={{0,1},{1,2},{2,3},{3,4},{4,5},{5,6},{6,7},{7,8},{8,9},{9,10},{10,1... | collective-permute-start | bytes 98312 | tf_op jit(solution)/shard_map/ppermute | solution.py:14
  96.9 12.5 %collective-permute-start.3 = (bf16[32,512]{1,0:T(8,128)(2,1)S(1)}, bf16[32,512]{1,0:T(8,128)(2,1)S(1)}, u32[]{:S(2)}, u32[]{:S(2)}) collective-permute-start(bf16[32,512]{1,0:T(8,128)(2,1)S(1)} %gather_fusion.5), channel_id=1, source_target_pairs={{1,0},{2,1},{3,2},{4,3},{5,4},{6,5},{7,6},{8,7},{9,8},{10,9},{11,1... | collective-permute-start | bytes 98312 | tf_op jit(solution)/shard_map/ppermute | solution.py:15
  110.8 8.9 %copy-start.3 = (bf16[2048,512]{0,1:T(8,128)(2,1)S(1)}, bf16[2048,512]{0,1:T(8,128)(2,1)}, u32[]{:S(2)}) copy-start(bf16[2048,512]{0,1:T(8,128)(2,1)} %add_convert_fusion.1) | copy-start | bytes 6291460
  119.8 8.7 %copy-start.6 = (f32[256,512]{1,0:T(8,128)S(1)}, f32[256,512]{1,0:T(8,128)}, u32[]{:S(2)}) copy-start(f32[256,512]{1,0:T(8,128)} %fusion.28) | copy-start | bytes 1572868
  119.8 8.7 %copy-start.15 = (s32[2048]{0:T(1024)S(1)}, s32[2048]{0:T(1024)}, u32[]{:S(2)}) copy-start(s32[2048]{0:T(1024)} %param.27) | copy-start | bytes 24580
  119.8 8.7 %copy-start.23 = (f32[1,512]{1,0:T(1,128)S(1)}, f32[1,512]{1,0:T(1,128)}, u32[]{:S(2)}) copy-start(f32[1,512]{1,0:T(1,128)} %get-tuple-element.9) | copy-start | bytes 6148
  128.5 6.0 %copy-start.10 = (f32[1,512]{1,0:T(1,128)S(1)}, f32[1,512]{1,0:T(1,128)}, u32[]{:S(2)}) copy-start(f32[1,512]{1,0:T(1,128)} %get-tuple-element.7) | copy-start | bytes 6148
  128.5 7.4 %copy-start.9 = (s32[1024]{0:T(1024)S(1)}, s32[1024]{0:T(1024)}, u32[]{:S(2)}) copy-start(s32[1024]{0:T(1024)} %pad_clamp_fusion.1) | copy-start | bytes 12292
  133.0 14.7 %copy-start.20 = (s32[256,1]{0,1:T(1,128)S(1)}, s32[256,1]{0,1:T(1,128)}, u32[]{:S(2)}) copy-start(s32[256,1]{0,1:T(1,128)} %copy-done.19) | copy-start | bytes 3076
  136.0 27.3 %copy-start.2 = (f32[256,512]{1,0:T(8,128)S(1)}, f32[256,512]{1,0:T(8,128)}, u32[]{:S(2)}) copy-start(f32[256,512]{1,0:T(8,128)} %copy-done.1) | copy-start | bytes 1572868
  136.0 27.3 %copy-start.8 = (bf16[256,227]{0,1:T(8,128)(2,1)S(1)}, bf16[256,227]{0,1:T(8,128)(2,1)}, u32[]{:S(2)}) copy-start(bf16[256,227]{0,1:T(8,128)(2,1)} %param.21) | copy-start | bytes 348676
  136.0 27.3 %copy-start.24 = (bf16[512,512]{1,0:T(8,128)(2,1)S(1)}, bf16[512,512]{1,0:T(8,128)(2,1)}, u32[]{:S(2)}) copy-start(bf16[512,512]{1,0:T(8,128)(2,1)} %param.40) | copy-start | bytes 1572868
  136.0 27.3 %copy-start.25 = (bf16[512,227]{0,1:T(8,128)(2,1)S(1)}, bf16[512,227]{0,1:T(8,128)(2,1)}, u32[]{:S(2)}) copy-start(bf16[512,227]{0,1:T(8,128)(2,1)} %param.41) | copy-start | bytes 697348
  138.6 23.5 %all-to-all-start.2 = ((bf16[16,32,512]{2,1,0:T(8,128)(2,1)}), bf16[16,32,512]{2,1,0:T(8,128)(2,1)S(1)}, u32[]{:S(2)}, u32[]{:S(2)}) async-start(bf16[16,32,512]{2,1,0:T(8,128)(2,1)} %bitcast.29), calls=%async_computation.2 | async-start | bytes 1048576 | tf_op jit(solution)/shard_map/all_to_all | solution.py:134
where the time goes:
time: 166 us; the launch traced here: 165 us
  local copies, waits for them, and re-layouts  51.1 us (31%)
  matrix products  42.9 us (26%)
  starting transfers between devices  30.2 us (18%)
  waiting for transfers between devices  26.4 us (16%)
  other arithmetic  13.5 us (8%)
    gather x2, local copies, waits for them, and re-layouts, shards(): from_sender[edge_sender]  17.8 us
    gather x2, local copies, waits for them, and re-layouts, shards(): from_receiver[edge_receiver]  17.8 us
    dot_general x2, matrix products, shards(): jnp.dot(edge_hidden, w_edge_out[depth], preferred_element_type=f32)  17.8 us
    all_to_all x1, waiting for transfers between devices, shards(): lax.all_to_all(reply_rows, 'band', split_axis=0, concat_axis=0, tiled=True)  14.4 us
    all_to_all x1, waiting for transfers between devices, shards(): lax.all_to_all(send_rows.reshape(part_count, capacity, latent_width), 'ba...  11.9 us
    all_to_all x1, starting transfers between devices, shards(): lax.all_to_all(reply_rows, 'band', split_axis=0, concat_axis=0, tiled=True)  9.02 us
    all_to_all x1, starting transfers between devices, shards(): lax.all_to_all(send_ids.reshape(part_count, capacity), 'band', split_axis...  7.37 us
    dot_general x2, matrix products, shards(): jnp.dot(edge_sum, node_weight[latent_width:], preferred_element_type=f32)  7.26 us
  transfers between devices with their start and end apart: 7, of which 2 were waited for; matrix products, arithmetic and copies ran while one was open for 22% of the time, Pallas kernels for 0%

commit v1 on v0

v1 whole, which is shorter than its diff:
```python
import functools

import jax
import jax.numpy as jnp
from jax import lax
from jax.experimental import pallas as pl
from jax.experimental.pallas import tpu as pltpu
from jax.sharding import PartitionSpec as P

F32 = jnp.float32
BF16 = jnp.bfloat16
MESH_ID = pl.DeviceIdType.MESH


def mm(a, b):
    return jnp.dot(a, b, preferred_element_type=F32)


def silu(v):
    return (0.5 * v) * (1.0 + jnp.tanh(0.5 * v))


def rms_norm(values, gain):
    return values * lax.rsqrt(jnp.mean(values * values, -1, keepdims=True) + 1e-05) * gain


def hot(condition):
    return jnp.where(condition, 1.0, 0.0).astype(BF16)


def iota(shape, axis):
    return lax.broadcasted_iota(jnp.int32, shape, axis)


def kernel(
    sizes,
    feats,
    owner,
    node,
    sender,
    receiver,
    low,
    high,
    gain_enc,
    gain_edge,
    gain_node,
    w_embed,
    w_out,
    mesh_feat_hbm,
    edge_hbm,
    w_g2m_hbm,
    w_edge_in_hbm,
    w_edge_out_hbm,
    w_node_in_hbm,
    w_node_out_hbm,
    w_mm_hbm,
    w_mg_hbm,
    out,
    x_pad,
    emb_pad,
    out_pad,
    mesh_feat,
    edges,
    w_g2m,
    w_edge_in,
    w_edge_out,
    w_node_in,
    w_node_out,
    w_mm,
    w_mg,
    send,
    recv,
    reply,
    back,
    unpack,
    gterm,
    pre,
    onehot,
    rhot,
    table,
    border,
    total,
    state,
    load_sem,
    a_send,
    a_recv,
    b_send,
    b_recv,
    h_send,
    h_recv,
):
    n, cap, chunk, tile = sizes
    me = lax.axis_index("band")
    grid_rows, channels = feats.shape
    width = x_pad.shape[1]
    mesh_rows, latent = mesh_feat.shape
    layers = w_edge_in.shape[0]
    slots = n * cap
    peers = chunk // cap
    rim = low.shape[1]
    tiles = edges.shape[0] // tile
    own0 = mesh_rows
    prev0 = 2 * mesh_rows
    next0 = prev0 + rim

    table[:, prev0:, :] = jnp.zeros(
        (layers, table.shape[1] - prev0, latent), BF16
    )

    barrier = pltpu.get_barrier_semaphore()

    def greet(k, c):
        pl.semaphore_signal(
            barrier,
            inc=1,
            device_id={"band": lax.rem(me + k, n)},
            device_id_type=MESH_ID,
        )
        return c

    lax.fori_loop(1, n, greet, 0)

    loads = [
        pltpu.make_async_copy(src, dst, load_sem.at[i])
        for i, (src, dst) in enumerate(
            (
                (w_edge_in_hbm, w_edge_in),
                (edge_hbm, edges),
                (w_g2m_hbm, w_g2m),
                (mesh_feat_hbm, mesh_feat),
                (w_edge_out_hbm, w_edge_out),
                (w_node_in_hbm, w_node_in),
                (w_node_out_hbm, w_node_out),
                (w_mg_hbm, w_mg),
                (w_mm_hbm, w_mm),
            )
        )
    ]
    for load in loads:
        load.start()

    owner_row = owner[...]
    owner_hot = owner_row == iota((n, grid_rows), 0)
    before = hot(iota((grid_rows, grid_rows), 0) < iota((grid_rows, grid_rows), 1))
    ranks = mm(hot(owner_hot), before)
    rank_row = jnp.sum(jnp.where(owner_hot, ranks, 0.0), 0, keepdims=True)
    flat_row = owner_row * cap + rank_row.astype(jnp.int32)
    flat_col = jnp.transpose(
        jnp.broadcast_to(flat_row.astype(F32), (8, grid_rows))
    )[:, 0:1]
    node_col = jnp.transpose(
        jnp.broadcast_to(node[...].astype(F32), (8, grid_rows))
    )[:, 0:1]
    x_pad[...] = jnp.zeros(x_pad.shape, BF16)
    x_pad[:, :channels] = feats[...]
    rows = jnp.where(
        iota((grid_rows, width), 1) == channels, node_col + 1.0, x_pad[...].astype(F32)
    ).astype(BF16)
    for c in range(slots // chunk):
        pick = hot(iota((chunk, grid_rows), 0) + c * chunk == flat_row)
        send[c * peers : (c + 1) * peers] = (
            mm(pick, rows).astype(BF16).reshape(peers, cap, width)
        )

    pl.semaphore_wait(barrier, n - 1)

    def to_owner(k):
        peer = lax.rem(me + k, n)
        return pltpu.make_async_remote_copy(
            src_ref=send.at[peer],
            dst_ref=recv.at[me],
            send_sem=a_send.at[peer],
            recv_sem=a_recv.at[me],
            device_id={"band": peer},
            device_id_type=MESH_ID,
        )

    def from_source(k):
        peer = lax.rem(me + k, n)
        return pltpu.make_async_remote_copy(
            src_ref=send.at[me],
            dst_ref=recv.at[peer],
            send_sem=a_send.at[me],
            recv_sem=a_recv.at[peer],
            device_id={"band": peer},
            device_id_type=MESH_ID,
        )

    def start_a(k, c):
        to_owner(k).start()
        return c

    lax.fori_loop(1, n, start_a, 0)
    recv[me] = send[me]

    unpack[...] = hot(iota((grid_rows, slots), 1).astype(F32) == flat_col)
    emb_pad[...] = jnp.zeros(emb_pad.shape, BF16)
    emb_pad[:channels, :] = w_embed[...]
    out_pad[...] = jnp.zeros(out_pad.shape, BF16)
    out_pad[:, :channels] = w_out[...]

    send_cols = jnp.transpose(sender[...].astype(F32))
    recv_cols = jnp.transpose(receiver[...].astype(F32))
    lanes = send_cols.shape[0]
    spare = onehot.shape[1] - mesh_rows
    lane_r = iota((lanes, mesh_rows), 1).astype(F32)
    lane_s = iota((lanes, spare), 1).astype(F32)
    for j in range(send_cols.shape[1]):
        at = slice(j * lanes, (j + 1) * lanes)
        onehot[at, :mesh_rows] = hot(recv_cols[:, j : j + 1] == lane_r)
        onehot[at, mesh_rows:] = hot(send_cols[:, j : j + 1] == lane_s)
    per = tile // lanes
    sub = iota((mesh_rows, lanes), 0)
    for j in range(send_cols.shape[1]):
        rhot[j // per, :, (j % per) * lanes : (j % per + 1) * lanes] = hot(
            receiver[j : j + 1, :] == sub
        )

    square = iota((rim, rim), 0) == iota((rim, rim), 1)
    low_col = jnp.sum(jnp.where(square, low[...].astype(F32), 0.0), 1, keepdims=True)
    high_col = jnp.sum(jnp.where(square, high[...].astype(F32), 0.0), 1, keepdims=True)
    rim_lane = iota((rim, mesh_rows), 1).astype(F32)
    low_hot = hot(low_col == rim_lane)
    high_hot = hot(high_col == rim_lane)

    loads[0].wait()
    loads[1].wait()

    def own_term(depth):
        def body(t, c):
            at = pl.ds(pl.multiple_of(t * tile, tile), tile)
            pre[at, :] = mm(edges[at, :], w_edge_in[depth, :latent, :])
            return c

        lax.fori_loop(0, tiles, body, 0)

    own_term(0)
    for load in loads[2:]:
        load.wait()

    def arrive_a(k, c):
        from_source(k).wait_recv()
        return c

    lax.fori_loop(1, n, arrive_a, 0)

    mark = hot(iota((16, width), 1) == channels)
    total[...] = jnp.zeros(total.shape, F32)

    def block(c):
        return recv[pl.ds(c * peers, peers)].reshape(chunk, width)

    for c in range(slots // chunk):
        got = block(c)
        ids = lax.dot_general(
            mark, got, (((1,), (1,)), ((), ())), preferred_element_type=F32
        )[0:1, :]
        pick = hot(ids == (iota((mesh_rows, chunk), 0) + 1).astype(F32))
        lat = silu(mm(got, emb_pad[...])).astype(BF16)
        gterm[c * chunk : (c + 1) * chunk, :] = lat
        total[...] += mm(pick, lat)
    encoded = total[...].astype(BF16)
    state[...] = (
        mesh_feat[...].astype(F32) + rms_norm(mm(encoded, w_g2m[...]), gain_enc[...])
    ).astype(BF16)

    def border_copy(depth, up):
        peer = lax.rem(me + 1, n) if up else lax.rem(me + n - 1, n)
        first = prev0 if up else next0
        return pltpu.make_async_remote_copy(
            src_ref=border.at[depth, int(up)],
            dst_ref=table.at[depth, pl.ds(first, rim)],
            send_sem=h_send.at[depth, int(up)],
            recv_sem=h_recv.at[depth, int(up)],
            device_id={"band": peer},
            device_id_type=MESH_ID,
        )

    for depth in range(layers):
        own = mm(state[...], w_edge_in[depth, latent : 2 * latent, :]).astype(BF16)
        border[depth, 0] = mm(low_hot, own).astype(BF16)
        border[depth, 1] = mm(high_hot, own).astype(BF16)

        @pl.when(me < n - 1)
        def _():
            border_copy(depth, True).start()

        @pl.when(me > 0)
        def _():
            border_copy(depth, False).start()

        table[depth, own0:prev0, :] = own
        table[depth, :own0, :] = mm(
            state[...], w_edge_in[depth, 2 * latent :, :]
        ).astype(BF16)
        if depth > 0:
            own_term(depth)
        total[...] = jnp.zeros(total.shape, F32)

        @pl.when(me > 0)
        def _():
            border_copy(depth, True).wait_recv()

        @pl.when(me < n - 1)
        def _():
            border_copy(depth, False).wait_recv()

        def edge_step(t, c):
            at = pl.ds(pl.multiple_of(t * tile, tile), tile)
            hidden = silu(pre[at, :] + mm(onehot[at, :], table[depth])).astype(BF16)
            now = (
                edges[at, :].astype(F32)
                + rms_norm(mm(hidden, w_edge_out[depth]), gain_edge[depth : depth + 1, :])
            ).astype(BF16)
            if depth < layers - 1:
                edges[at, :] = now
            total[...] += mm(rhot[t], now)
            return c

        lax.fori_loop(0, tiles, edge_step, 0)
        summed = total[...].astype(BF16)
        hidden = silu(
            mm(state[...], w_node_in[depth, :latent, :])
            + mm(summed, w_node_in[depth, latent:, :])
        ).astype(BF16)
        state[...] = (
            state[...].astype(F32)
            + rms_norm(mm(hidden, w_node_out[depth]), gain_node[depth : depth + 1, :])
        ).astype(BF16)

    term = mm(state[...], w_mm[...]).astype(BF16)

    def to_source(peer):
        return pltpu.make_async_remote_copy(
            src_ref=reply.at[peer],
            dst_ref=back.at[me],
            send_sem=b_send.at[peer],
            recv_sem=b_recv.at[me],
            device_id={"band": peer},
            device_id_type=MESH_ID,
        )

    def from_owner(peer):
        return pltpu.make_async_remote_copy(
            src_ref=reply.at[me],
            dst_ref=back.at[peer],
            send_sem=b_send.at[me],
            recv_sem=b_recv.at[peer],
            device_id={"band": peer},
            device_id_type=MESH_ID,
        )

    for c in range(slots // chunk):
        got = block(c).astype(F32)
        pick = hot(
            got[:, channels : channels + 1] == (iota((chunk, mesh_rows), 1) + 1).astype(F32)
        )
        lat = gterm[c * chunk : (c + 1) * chunk, :]
        dec = silu(mm(pick, term) + mm(lat, w_mg[...])).astype(BF16)
        reply[c * peers : (c + 1) * peers] = (
            (got + mm(dec, out_pad[...])).astype(BF16).reshape(peers, cap, width)
        )

        def start_b(peer, k):
            @pl.when(peer != me)
            def _():
                to_source(peer).start()

            return k

        lax.fori_loop(c * peers, (c + 1) * peers, start_b, 0)
    back[me] = reply[me]

    def arrive_b(k, c):
        from_owner(lax.rem(me + k, n)).wait_recv()
        return c

    lax.fori_loop(1, n, arrive_b, 0)
    result = mm(unpack[...], back[...].reshape(slots, width)).astype(BF16)
    out[...] = result[:, :channels]

    def sent(k, c):
        to_owner(k).wait_send()
        to_source(lax.rem(me + k, n)).wait_send()
        return c

    lax.fori_loop(1, n, sent, 0)
    for depth in range(layers):

        @pl.when(me < n - 1)
        def _():
            border_copy(depth, True).wait_send()

        @pl.when(me > 0)
        def _():
            border_copy(depth, False).wait_send()


def round_up(value, step):
    return -(-value // step) * step


def shards(
    grid_feats,
    mesh_feat,
    edge_latent,
    g2m_owner,
    g2m_node,
    edge_sender,
    edge_receiver,
    border_low,
    border_high,
    w_embed,
    w_g2m,
    gain_enc,
    w_edge_in,
    w_edge_out,
    gain_edge,
    w_node_in,
    w_node_out,
    gain_node,
    w_m2g_mesh,
    w_m2g_grid,
    w_out,
):
    n = lax.axis_size("band")
    grid_rows, channels = grid_feats.shape
    mesh_rows, latent = mesh_feat.shape
    edge_rows = edge_latent.shape[0]
    layers = w_edge_in.shape[0]
    rim = border_low.shape[1]
    cap = round_up(2 * grid_rows // n, 16)
    slots = n * cap
    chunk = min(slots, 256)
    tile = min(edge_rows, 512)
    width = round_up(channels + 1, 128)
    table_rows = round_up(2 * mesh_rows + 2 * rim, 128)
    vmem = pl.BlockSpec(memory_space=pltpu.VMEM)
    hbm = pl.BlockSpec(memory_space=pl.ANY)

    def like(a):
        return pltpu.VMEM(a.shape, a.dtype)

    dma = pltpu.SemaphoreType.DMA
    return pl.pallas_call(
        functools.partial(kernel, (n, cap, chunk, tile)),
        out_shape=jax.ShapeDtypeStruct((grid_rows, channels), BF16),
        in_specs=[vmem] * 12 + [hbm] * 9,
        out_specs=vmem,
        scratch_shapes=[
            pltpu.VMEM((grid_rows, width), BF16),
            pltpu.VMEM((width, latent), BF16),
            pltpu.VMEM((latent, width), BF16),
            like(mesh_feat),
            like(edge_latent),
            like(w_g2m),
            like(w_edge_in),
            like(w_edge_out),
            like(w_node_in),
            like(w_node_out),
            like(w_m2g_mesh),
            like(w_m2g_grid),
            pltpu.VMEM((n, cap, width), BF16),
            pltpu.VMEM((n, cap, width), BF16),
            pltpu.VMEM((n, cap, width), BF16),
            pltpu.VMEM((n, cap, width), BF16),
            pltpu.VMEM((grid_rows, slots), BF16),
            pltpu.VMEM((slots, latent), BF16),
            pltpu.VMEM((edge_rows, latent), F32),
            pltpu.VMEM((edge_rows, table_rows), BF16),
            pltpu.VMEM((edge_rows // tile, mesh_rows, tile), BF16),
            pltpu.VMEM((layers, table_rows, latent), BF16),
            pltpu.VMEM((layers, 2, rim, latent), BF16),
            pltpu.VMEM((mesh_rows, latent), F32),
            pltpu.VMEM((mesh_rows, latent), BF16),
            dma((9,)),
            dma((n,)),
            dma((n,)),
            dma((n,)),
            dma((n,)),
            dma((layers, 2)),
            dma((layers, 2)),
        ],
        compiler_params=pltpu.CompilerParams(
            collective_id=0, has_side_effects=True, vmem_limit_bytes=56 * 1024 * 1024
        ),
        cost_estimate=pl.CostEstimate(
            flops=10_000_000_000, bytes_accessed=16_000_000, transcendentals=3_000_000
        ),
    )(
        grid_feats,
        g2m_owner.reshape(1, grid_rows),
        g2m_node.reshape(1, grid_rows),
        edge_sender.reshape(edge_rows // 128, 128),
        edge_receiver.reshape(edge_rows // 128, 128),
        border_low,
        border_high,
        gain_enc.reshape(1, latent),
        gain_edge,
        gain_node,
        w_embed,
        w_out,
        mesh_feat,
        edge_latent,
        w_g2m,
        w_edge_in,
        w_edge_out,
        w_node_in,
        w_node_out,
        w_m2g_mesh,
        w_m2g_grid,
    )


def solution(mesh):
    return jax.shard_map(
        shards,
        mesh=mesh,
        in_specs=(
            P(("groups", "band"), None),
            P("band", None),
            P("band", None),
            P("band", None),
            P("band"),
            P("band"),
            P("band"),
            P("band", None),
            P("band", None),
        )
        + (P(),) * 12,
        out_specs=P(("groups", "band"), None),
        check_vma=False,
    )
```

time: 166 us -> 46.8 us (0.28)
  the two profiles are of different devices: /device:TPU:0 before, /device:TPU:25 now
where the time goes in v1:
time: 46.8 us; the launch traced here: 46.6 us
  Pallas kernels  41.5 us (89%)
  local copies, waits for them, and re-layouts  5.09 us (11%)
    pallas_call x1, Pallas kernels, shards(): pl.pallas_call(functools.partial(kernel, (n, cap, chunk, tile)), out_shap...  41.5 us
    unnamed x2, local copies, waits for them, and re-layouts  3.43 us
    pallas_call x1, local copies, waits for them, and re-layouts, shards(): pl.pallas_call(functools.partial(kernel, (n, cap, chunk, tile)), out_shap...  1.66 us

profile of v1, /device:TPU:25, one launch (start us, length us, event | category | flops | bytes accessed | tf_op | source)
XLA Modules:
  0.0 46.6 jit_solution(16764847969127644891)
XLA Ops:
  0.0 1.7 %copy.22.feats = bf16[256,227]{1,0:T(8,128)(2,1)} copy(bf16[256,227]{0,1:T(8,128)(2,1)} %param.21) | data formatting | bytes 232448 | tf_op args[0]
  1.7 1.8 %copy.23.w_out = bf16[512,227]{1,0:T(8,128)(2,1)} copy(bf16[512,227]{0,1:T(8,128)(2,1)} %param.41) | data formatting | bytes 464896 | tf_op args[20]
  3.4 41.5 %shard_map.199 = bf16[256,227]{1,0:T(8,128)(2,1)} custom-call(bf16[256,227]{1,0:T(8,128)(2,1)} %copy.22.feats, s32[1,256]{1,0:T(1,128)} %bitcast.8, s32[1,256]{1,0:T(1,128)} %bitcast.9, s32[16,128]{1,0:T(8,128)} %bitcast.5, s32[16,128]{1,0:T(8,128)} %bitcast.6, s32[1,32]{1,0:T(1,128)} %low.1, s32[1,32]{1,0:T(1,128)} %high.1, f32[1,512]{1,0:T(1,128)} %bitcast.7, ...), custom_call_target="tpu_custom_call" | custom-call | flops 10000000000 | bytes 16000000 | tf_op jit(solution)/shard_map/pallas_call | solution.py:445
  45.0 1.7 %copy.24 = bf16[256,227]{0,1:T(8,128)(2,1)} copy(bf16[256,227]{1,0:T(8,128)(2,1)} %shard_map.199) | data formatting | bytes 232448 | tf_op jit(solution)/shard_map/pallas_call | solution.py:445

commit v2 on v1

--- a/solution.py
+++ b/solution.py
@@ -14,6 +14,10 @@
 
 def mm(a, b):
     return jnp.dot(a, b, preferred_element_type=F32)
+
+
+def mm_t(a, b):
+    return lax.dot_general(a, b, (((1,), (1,)), ((), ())), preferred_element_type=F32)
 
 
 def silu(v):
@@ -73,6 +77,7 @@
     reply,
     back,
     unpack,
+    lats,
     gterm,
     pre,
     onehot,
@@ -91,8 +96,8 @@
 ):
     n, cap, chunk, tile = sizes
     me = lax.axis_index("band")
-    grid_rows, channels = feats.shape
-    width = x_pad.shape[1]
+    channels, grid_rows = feats.shape
+    width = x_pad.shape[0]
     mesh_rows, latent = mesh_feat.shape
     layers = w_edge_in.shape[0]
     slots = n * cap
@@ -148,24 +153,30 @@
     flat_col = jnp.transpose(
         jnp.broadcast_to(flat_row.astype(F32), (8, grid_rows))
     )[:, 0:1]
-    node_col = jnp.transpose(
-        jnp.broadcast_to(node[...].astype(F32), (8, grid_rows))
-    )[:, 0:1]
     x_pad[...] = jnp.zeros(x_pad.shape, BF16)
-    x_pad[:, :channels] = feats[...]
-    rows = jnp.where(
-        iota((grid_rows, width), 1) == channels, node_col + 1.0, x_pad[...].astype(F32)
+    x_pad[:channels, :] = feats[...]
+    columns = jnp.where(
+        iota((width, grid_rows), 0) == channels,
+        node[...].astype(F32) + 1.0,
+        x_pad[...].astype(F32),
     ).astype(BF16)
     for c in range(slots // chunk):
         pick = hot(iota((chunk, grid_rows), 0) + c * chunk == flat_row)
         send[c * peers : (c + 1) * peers] = (
-            mm(pick, rows).astype(BF16).reshape(peers, cap, width)
+            mm_t(pick, columns).astype(BF16).reshape(peers, cap, width)
         )
 
     pl.semaphore_wait(barrier, n - 1)
 
+    half = n // 2
+
+    def partner(k):
+        far = lax.rem((me // half + 1) * half + lax.rem(me + k, half), n)
+        near = (me // half) * half + lax.rem(me + k - half, half)
+        return jnp.where(k < half, far, near)
+
     def to_owner(k):
-        peer = lax.rem(me + k, n)
+        peer = partner(k)
         return pltpu.make_async_remote_copy(
             src_ref=send.at[peer],
             dst_ref=recv.at[me],
@@ -176,7 +187,7 @@
         )
 
     def from_source(k):
-        peer = lax.rem(me + k, n)
+        peer = partner(k)
         return pltpu.make_async_remote_copy(
             src_ref=send.at[me],
             dst_ref=recv.at[peer],
@@ -186,18 +197,22 @@
             device_id_type=MESH_ID,
         )
 
+    def others(step):
+        lax.fori_loop(0, half, step, 0)
+        lax.fori_loop(half + 1, n, step, 0)
+
     def start_a(k, c):
         to_owner(k).start()
         return c
 
-    lax.fori_loop(1, n, start_a, 0)
+    others(start_a)
     recv[me] = send[me]
 
     unpack[...] = hot(iota((grid_rows, slots), 1).astype(F32) == flat_col)
     emb_pad[...] = jnp.zeros(emb_pad.shape, BF16)
     emb_pad[:channels, :] = w_embed[...]
     out_pad[...] = jnp.zeros(out_pad.shape, BF16)
-    out_pad[:, :channels] = w_out[...]
+    out_pad[:channels, :] = w_out[...]
 
     send_cols = jnp.transpose(sender[...].astype(F32))
     recv_cols = jnp.transpose(receiver[...].astype(F32))
@@ -234,15 +249,25 @@
 
         lax.fori_loop(0, tiles, body, 0)
 
+    def inner_term(depth):
+        def body(t, c):
+            at = pl.ds(pl.multiple_of(t * tile, tile), tile)
+            inner = mm(onehot[at, :prev0], table[depth, :prev0, :])
+            if depth == 0:
+                pre[at, :] += inner
+            else:
+                pre[at, :] = inner + mm(edges[at, :], w_edge_in[depth, :latent, :])
+            return c
+
+        lax.fori_loop(0, tiles, body, 0)
+
     own_term(0)
-    for load in loads[2:]:
-        load.wait()
 
     def arrive_a(k, c):
         from_source(k).wait_recv()
         return c
 
-    lax.fori_loop(1, n, arrive_a, 0)
+    others(arrive_a)
 
     mark = hot(iota((16, width), 1) == channels)
     total[...] = jnp.zeros(total.shape, F32)
@@ -252,14 +277,14 @@
 
     for c in range(slots // chunk):
         got = block(c)
-        ids = lax.dot_general(
-            mark, got, (((1,), (1,)), ((), ())), preferred_element_type=F32
-        )[0:1, :]
+        ids = mm_t(mark, got)[0:1, :]
         pick = hot(ids == (iota((mesh_rows, chunk), 0) + 1).astype(F32))
         lat = silu(mm(got, emb_pad[...])).astype(BF16)
-        gterm[c * chunk : (c + 1) * chunk, :] = lat
+        lats[c * chunk : (c + 1) * chunk, :] = lat
         total[...] += mm(pick, lat)
     encoded = total[...].astype(BF16)
+    for load in loads[2:4]:
+        load.wait()
     state[...] = (
         mesh_feat[...].astype(F32) + rms_norm(mm(encoded, w_g2m[...]), gain_enc[...])
     ).astype(BF16)
@@ -276,6 +301,8 @@
             device_id_type=MESH_ID,
         )
 
+    for load in loads[4:]:
+        load.wait()
     for depth in range(layers):
         own = mm(state[...], w_edge_in[depth, latent : 2 * latent, :]).astype(BF16)
         border[depth, 0] = mm(low_hot, own).astype(BF16)
@@ -293,8 +320,11 @@
         table[depth, :own0, :] = mm(
             state[...], w_edge_in[depth, 2 * latent :, :]
         ).astype(BF16)
-        if depth > 0:
-            own_term(depth)
+        inner_term(depth)
+        if depth == 0:
+            for c in range(slots // chunk):
+                at = slice(c * chunk, (c + 1) * chunk)
+                gterm[at, :] = mm(lats[at, :], w_mg[...])
         total[...] = jnp.zeros(total.shape, F32)
 
         @pl.when(me > 0)
@@ -307,7 +337,9 @@
 
         def edge_step(t, c):
             at = pl.ds(pl.multiple_of(t * tile, tile), tile)
-            hidden = silu(pre[at, :] + mm(onehot[at, :], table[depth])).astype(BF16)
+            hidden = silu(
+                pre[at, :] + mm(onehot[at, prev0:], table[depth, prev0:, :])
+            ).astype(BF16)
             now = (
                 edges[at, :].astype(F32)
                 + rms_norm(mm(hidden, w_edge_out[depth]), gain_edge[depth : depth + 1, :])
@@ -350,41 +382,45 @@
             device_id_type=MESH_ID,
         )
 
-    for c in range(slots // chunk):
+    chunks = slots // chunk
+    for step in range(chunks):
+        c = lax.rem(me // peers + step + (chunks + 1) // 2, chunks)
         got = block(c).astype(F32)
         pick = hot(
             got[:, channels : channels + 1] == (iota((chunk, mesh_rows), 1) + 1).astype(F32)
         )
-        lat = gterm[c * chunk : (c + 1) * chunk, :]
-        dec = silu(mm(pick, term) + mm(lat, w_mg[...])).astype(BF16)
-        reply[c * peers : (c + 1) * peers] = (
-            (got + mm(dec, out_pad[...])).astype(BF16).reshape(peers, cap, width)
-        )
-
-        def start_b(peer, k):
+        at = pl.ds(pl.multiple_of(c * chunk, chunk), chunk)
+        dec = silu(mm(pick, term) + gterm[at, :]).astype(BF16)
+        reply[pl.ds(c * peers, peers)] = (
+            (got + mm_t(dec, out_pad[...])).astype(BF16).reshape(peers, cap, width)
+        )
+
+        def start_b(j, k):
+            peer = c * peers + lax.rem(me + j, peers)
+
             @pl.when(peer != me)
             def _():
                 to_source(peer).start()
 
             return k
 
-        lax.fori_loop(c * peers, (c + 1) * peers, start_b, 0)
+        lax.fori_loop(0, peers, start_b, 0)
     back[me] = reply[me]
 
     def arrive_b(k, c):
-        from_owner(lax.rem(me + k, n)).wait_recv()
+        from_owner(partner(k)).wait_recv()
         return c
 
-    lax.fori_loop(1, n, arrive_b, 0)
-    result = mm(unpack[...], back[...].reshape(slots, width)).astype(BF16)
-    out[...] = result[:, :channels]
+    others(arrive_b)
+    result = jnp.transpose(mm(unpack[...], back[...].reshape(slots, width)))
+    out[...] = result.astype(BF16)[:channels, :]
 
     def sent(k, c):
         to_owner(k).wait_send()
-        to_source(lax.rem(me + k, n)).wait_send()
+        to_source(partner(k)).wait_send()
         return c
 
-    lax.fori_loop(1, n, sent, 0)
+    others(sent)
     for depth in range(layers):
 
         @pl.when(me < n - 1)
@@ -444,13 +480,13 @@
     dma = pltpu.SemaphoreType.DMA
     return pl.pallas_call(
         functools.partial(kernel, (n, cap, chunk, tile)),
-        out_shape=jax.ShapeDtypeStruct((grid_rows, channels), BF16),
+        out_shape=jax.ShapeDtypeStruct((channels, grid_rows), BF16),
         in_specs=[vmem] * 12 + [hbm] * 9,
         out_specs=vmem,
         scratch_shapes=[
-            pltpu.VMEM((grid_rows, width), BF16),
+            pltpu.VMEM((width, grid_rows), BF16),
             pltpu.VMEM((width, latent), BF16),
-            pltpu.VMEM((latent, width), BF16),
+            pltpu.VMEM((width, latent), BF16),
             like(mesh_feat),
             like(edge_latent),
             like(w_g2m),
@@ -466,6 +502,7 @@
             pltpu.VMEM((n, cap, width), BF16),
             pltpu.VMEM((grid_rows, slots), BF16),
             pltpu.VMEM((slots, latent), BF16),
+            pltpu.VMEM((slots, latent), F32),
             pltpu.VMEM((edge_rows, latent), F32),
             pltpu.VMEM((edge_rows, table_rows), BF16),
             pltpu.VMEM((edge_rows // tile, mesh_rows, tile), BF16),
@@ -488,7 +525,7 @@
             flops=10_000_000_000, bytes_accessed=16_000_000, transcendentals=3_000_000
         ),
     )(
-        grid_feats,
+        grid_feats.T,
         g2m_owner.reshape(1, grid_rows),
         g2m_node.reshape(1, grid_rows),
         edge_sender.reshape(edge_rows // 128, 128),
@@ -499,7 +536,7 @@
         gain_edge,
         gain_node,
         w_embed,
-        w_out,
+        w_out.T,
         mesh_feat,
         edge_latent,
         w_g2m,
@@ -509,7 +546,7 @@
         w_node_out,
         w_m2g_mesh,
         w_m2g_grid,
-    )
+    ).T
 
 
 def solution(mesh):

time: 46.8 us -> 44.4 us (0.949)
  the two profiles are of different devices: /device:TPU:25 before, /device:TPU:0 now
where the time goes in v2:
time: 44.4 us; the launch traced here: 44.2 us
  Pallas kernels  42.7 us (96%)
  local copies, waits for them, and re-layouts  1.56 us (4%)
    pallas_call x1, Pallas kernels, shards(): pl.pallas_call(functools.partial(kernel, (n, cap, chunk, tile)), out_shap...  42.7 us
    unnamed x1, local copies, waits for them, and re-layouts  1.56 us

profile of v2, /device:TPU:0, one launch (start us, length us, event | category | flops | bytes accessed | tf_op | source)
XLA Modules:
  0.0 44.2 jit_solution(3645313255455123058)
XLA Ops:
  0.0 42.7 %shard_map.199 = bf16[227,256]{1,0:T(8,128)(2,1)} custom-call(bf16[227,256]{1,0:T(8,128)(2,1)} %bitcast.10, s32[1,256]{1,0:T(1,128)} %bitcast.14, s32[1,256]{1,0:T(1,128)} %bitcast.15, s32[16,128]{1,0:T(8,128)} %bitcast.11, s32[16,128]{1,0:T(8,128)} %bitcast.12, s32[1,32]{1,0:T(1,128)} %low.1, s32[1,32]{1,0:T(1,128)} %high.1, f32[1,512]{1,0:T(1,128)} %bitcast.13, ...), custom_call_target="tpu_custom_call" | custom-call | flops 10000000000 | bytes 16000000 | tf_op jit(solution)/shard_map/pallas_call | solution.py:481
  42.7 1.6 %copy.23 = bf16[256,227]{0,1:T(8,128)(2,1)} copy(bf16[256,227]{0,1:T(8,128)(2,1)} %bitcast.8) | data formatting | bytes 232448

commit v3 on v2

--- a/solution.py
+++ b/solution.py
@@ -168,12 +168,8 @@
 
     pl.semaphore_wait(barrier, n - 1)
 
-    half = n // 2
-
     def partner(k):
-        far = lax.rem((me // half + 1) * half + lax.rem(me + k, half), n)
-        near = (me // half) * half + lax.rem(me + k - half, half)
-        return jnp.where(k < half, far, near)
+        return lax.rem(me + k, n)
 
     def to_owner(k):
         peer = partner(k)
@@ -198,8 +194,7 @@
         )
 
     def others(step):
-        lax.fori_loop(0, half, step, 0)
-        lax.fori_loop(half + 1, n, step, 0)
+        lax.fori_loop(1, n, step, 0)
 
     def start_a(k, c):
         to_owner(k).start()
@@ -384,19 +379,19 @@
 
     chunks = slots // chunk
     for step in range(chunks):
-        c = lax.rem(me // peers + step + (chunks + 1) // 2, chunks)
+        c = step
         got = block(c).astype(F32)
         pick = hot(
             got[:, channels : channels + 1] == (iota((chunk, mesh_rows), 1) + 1).astype(F32)
         )
-        at = pl.ds(pl.multiple_of(c * chunk, chunk), chunk)
+        at = pl.ds(c * chunk, chunk)
         dec = silu(mm(pick, term) + gterm[at, :]).astype(BF16)
         reply[pl.ds(c * peers, peers)] = (
             (got + mm_t(dec, out_pad[...])).astype(BF16).reshape(peers, cap, width)
         )
 
         def start_b(j, k):
-            peer = c * peers + lax.rem(me + j, peers)
+            peer = c * peers + j
 
             @pl.when(peer != me)
             def _():
@@ -468,7 +463,7 @@
     cap = round_up(2 * grid_rows // n, 16)
     slots = n * cap
     chunk = min(slots, 256)
-    tile = min(edge_rows, 512)
+    tile = min(edge_rows, 2048)
     width = round_up(channels + 1, 128)
     table_rows = round_up(2 * mesh_rows + 2 * rim, 128)
     vmem = pl.BlockSpec(memory_space=pltpu.VMEM)

time: 44.4 us -> 38.8 us (0.87)
  the two profiles are of different devices: /device:TPU:0 before, /device:TPU:29 now
where the time goes in v3:
time: 38.8 us; the launch traced here: 38.7 us
  Pallas kernels  37.1 us (96%)
  local copies, waits for them, and re-layouts  1.56 us (4%)
    pallas_call x1, Pallas kernels, shards(): pl.pallas_call(functools.partial(kernel, (n, cap, chunk, tile)), out_shap...  37.1 us
    unnamed x1, local copies, waits for them, and re-layouts  1.56 us

profile of v3, /device:TPU:29, one launch (start us, length us, event | category | flops | bytes accessed | tf_op | source)
XLA Modules:
  0.0 38.7 jit_solution(589579147016331942)
XLA Ops:
  0.0 37.1 %shard_map.199 = bf16[227,256]{1,0:T(8,128)(2,1)} custom-call(bf16[227,256]{1,0:T(8,128)(2,1)} %bitcast.10, s32[1,256]{1,0:T(1,128)} %bitcast.14, s32[1,256]{1,0:T(1,128)} %bitcast.15, s32[16,128]{1,0:T(8,128)} %bitcast.11, s32[16,128]{1,0:T(8,128)} %bitcast.12, s32[1,32]{1,0:T(1,128)} %low.1, s32[1,32]{1,0:T(1,128)} %high.1, f32[1,512]{1,0:T(1,128)} %bitcast.13, ...), custom_call_target="tpu_custom_call" | custom-call | flops 10000000000 | bytes 16000000 | tf_op jit(solution)/shard_map/pallas_call | solution.py:476
  37.1 1.6 %copy.23 = bf16[256,227]{0,1:T(8,128)(2,1)} copy(bf16[256,227]{0,1:T(8,128)(2,1)} %bitcast.8) | data formatting | bytes 232448
